TPU v7x, 32 devices: a whole 2x2x4 slice. The times are simulated.
32 devices in a mesh: ctx: 4 (over y, x), tp: 8 (over z, core).
Axes of the slice: x: 2, y: 2, z: 4, core: 2. Of those that a mesh axis runs over, the one named last changes fastest.
Arguments:
- queries: bfloat16 [896, 8192], P('ctx', 'tp'), may hold values from -8 to 8
- keys: bfloat16 [896, 1024], P('ctx'), may hold values from -8 to 8
- values: bfloat16 [896, 1024], P('ctx'), may hold values from -32 to 32
- out_weight: bfloat16 [8192, 8192], P('tp'), may hold values from -0.09375 to 0.09375
- signs: int32 [8192], replicated, may hold values from 0 to 1
Outputs:
- rotated_payload: bfloat16 [896, 8192], P('ctx')
- block_scales: float32 [896, 64], P('ctx')
All inputs are finite; a program needn't handle non-finite values. Where the computation divides by a largest or mean magnitude, that divisor is 1e-20 or more.
Results may differ from a plain program's by a relative error of at most 0.0095.
Values may be sent and summed in bfloat16 or wider, within the bound.
A program may use at most 128 MiB of HBM per device.

v0:
```python
import math

import jax
import jax.numpy as jnp
from jax import lax
from jax.sharding import PartitionSpec as P

D = 8192
QUERY_HEADS = 64
KEY_VALUE_HEADS = 8
HEAD_SIZE = 128
BLOCK = 128


clip_ratio = 2.0


def plus_minus():
    indices = jnp.arange(BLOCK, dtype=jnp.int32)
    common = jnp.bitwise_and(indices[:, None], indices[None, :])
    parity = jnp.zeros((BLOCK, BLOCK), jnp.int32)
    for bit_index in range(BLOCK.bit_length() - 1):
        parity = parity + jnp.bitwise_and(jnp.right_shift(common, bit_index), 1)
    return (1 - 2 * (parity % 2)).astype(jnp.bfloat16)


def rotate(partial_value, sign_row):
    row_count = partial_value.shape[0]
    flat = (partial_value * sign_row[None, :]).reshape(-1, BLOCK)
    upper = flat.astype(jnp.bfloat16)
    lower = (flat - upper.astype(jnp.float32)).astype(jnp.bfloat16)
    matrix = plus_minus()
    turned = jnp.dot(upper, matrix, preferred_element_type=jnp.float32)
    turned = turned + jnp.dot(lower, matrix, preferred_element_type=jnp.float32)
    turned = turned * jnp.float32(1.0 / math.sqrt(BLOCK))
    return turned.reshape(row_count, partial_value.shape[1])


def clip_quantize(rotated):
    row_count = rotated.shape[0]
    blocked = rotated.reshape(row_count, -1, BLOCK)
    scales = clip_ratio * jnp.sqrt(jnp.mean(blocked * blocked, axis=-1) + 1e-06)
    payload = (
        jnp.clip(blocked / scales[..., None], -1.0, 1.0).astype(jnp.bfloat16).reshape(row_count, -1)
    )
    return (payload, scales)


def quantize(rotated):
    row_count = rotated.shape[0]
    blocked = rotated.reshape(row_count, -1, BLOCK)
    scales = jnp.max(jnp.abs(blocked), axis=-1) + 1e-06
    payload = (blocked / scales[..., None]).astype(jnp.bfloat16).reshape(row_count, -1)
    return (payload, scales)


def attend(query_sets, key_head, value_head, head_count):
    score_scale = 1.0 / math.sqrt(HEAD_SIZE)
    prepared = []
    initial = []
    for query_rows, positions in query_sets:
        row_count = query_rows.shape[0]
        prepared.append((query_rows.reshape(row_count, head_count, HEAD_SIZE), positions))
        initial.append(
            (
                jnp.full((head_count, row_count), -1e30, jnp.float32),
                jnp.zeros((head_count, row_count), jnp.float32),
                jnp.zeros((head_count, row_count, HEAD_SIZE), jnp.float32),
            )
        )
    carried = tuple(initial)
    offset = jnp.int32(0)
    key_piece = lax.all_gather(key_head, "ctx", axis=0, tiled=True)
    value_piece = lax.all_gather(value_head, "ctx", axis=0, tiled=True)
    value_wide = value_piece.astype(jnp.float32)
    key_pos = jnp.arange(key_piece.shape[0], dtype=jnp.int32)
    renewed = []
    for (absorb_query_heads, absorb_positions), running in zip(prepared, carried):

        def update(running_in):
            run_max, run_sum, run_acc = running_in
            scores = (
                jnp.einsum(
                    "rhd,nd->hrn", absorb_query_heads, key_piece, preferred_element_type=jnp.float32
                )
                * score_scale
            )
            allowed = key_pos[None, None, :] <= absorb_positions[None, :, None]
            scores = jnp.where(allowed, scores, -1e30)
            new_max = jnp.maximum(run_max, jnp.max(scores, axis=-1))
            weights = jnp.where(allowed, jnp.exp(scores - new_max[..., None]), 0.0)
            new_sum = jnp.sum(weights, axis=-1)
            mixed = jnp.einsum("hrn,nd->hrd", weights, value_wide, precision=lax.Precision.HIGHEST)
            return (new_max, new_sum, mixed)

        def unchanged(running_in):
            return running_in

        renewed.append(lax.cond(offset <= absorb_positions[-1], update, unchanged, running))
    finished = tuple(renewed)
    results = []
    for (query_heads, positions), (run_max, run_sum, run_acc) in zip(prepared, finished):
        normed = (run_acc / run_sum[..., None]).astype(jnp.bfloat16)
        results.append(
            jnp.transpose(normed, (1, 0, 2)).reshape(normed.shape[1], head_count * HEAD_SIZE)
        )
    return results


def local(queries, keys, values, out_weight, signs):
    row_count = queries.shape[0]
    head_count = queries.shape[1] // HEAD_SIZE
    group_width = QUERY_HEADS // KEY_VALUE_HEADS
    ctx_index = lax.axis_index("ctx")
    kv_index = lax.axis_index("tp") * head_count // group_width
    key_head = lax.dynamic_slice_in_dim(keys, kv_index * HEAD_SIZE, HEAD_SIZE, 1)
    value_head = lax.dynamic_slice_in_dim(values, kv_index * HEAD_SIZE, HEAD_SIZE, 1)
    first_pos = ctx_index * row_count
    query_sets = [(queries, first_pos + jnp.arange(row_count, dtype=jnp.int32))]
    attended = attend(query_sets, key_head, value_head, head_count)[0]
    partial_value = jnp.dot(attended, out_weight, preferred_element_type=jnp.float32)
    sign_row = (2 * signs - 1).astype(jnp.float32)
    payload, scales = clip_quantize(rotate(partial_value, sign_row))
    restored = payload.astype(jnp.float32).reshape(row_count, -1, BLOCK) * scales[..., None]
    summed = lax.psum_scatter(restored.reshape(row_count, D), "tp", scatter_dimension=1, tiled=True)
    out_payload, out_scales = quantize(summed)
    rotated_payload, block_scales = (
        lax.all_gather(out_payload, "tp", axis=1, tiled=True),
        lax.all_gather(out_scales.astype(jnp.bfloat16), "tp", axis=1, tiled=True).astype(
            out_scales.dtype
        ),
    )
    return (rotated_payload, block_scales)


def solution(mesh):
    return jax.shard_map(
        local,
        mesh=mesh,
        in_specs=(P("ctx", "tp"), P("ctx", None), P("ctx", None), P("tp", None), P()),
        out_specs=(P("ctx", None), P("ctx", None)),
        check_vma=False,
    )
```

profile of v0, /device:TPU:7, one launch (start us, length us, event | category | flops | bytes accessed | tf_op | source)
XLA Modules:
  0.0 244.3 jit_solution(740889643310335105)
XLA Ops:
  7.2 0.9 copy-done
  8.2 5.9 %all_gather.13 = bf16[896,128]{1,0:T(8,128)(2,1)S(1)} all-gather(bf16[224,128]{1,0:T(8,128)(2,1)S(1)} %constant_dynamic-slice_fusion), channel_id=1, replica_groups=mesh['ctx'=4,'tp'=8] {'ctx'}, dimensions={0}, use_global_device_ids=true | all-gather | bytes 286720 | tf_op jit(solution)/shard_map/all_gather | solution.py:74
  14.1 0.8 constant_dynamic-slice_fusion.1
  14.9 6.8 %all_gather.12 = bf16[896,128]{1,0:T(8,128)(2,1)S(1)} all-gather(bf16[224,128]{1,0:T(8,128)(2,1)S(1)} %constant_dynamic-slice_fusion.1), channel_id=1, replica_groups=mesh['ctx'=4,'tp'=8] {'ctx'}, dimensions={0}, use_global_device_ids=true | all-gather | bytes 286720 | tf_op jit(solution)/shard_map/all_gather | solution.py:73
  23.0 0.8 add_convert_fusion
  23.8 11.9 %conditional.1 = (f32[8,224]{1,0:T(8,128)S(1)}, f32[8,224,128]{2,1,0:T(8,128)S(1)}) conditional(s32[]{:T(128)} %bitcast.3, () %tuple.16, (s32[896]{0:T(1024)S(1)}, s32[224]{0:T(256)S(1)}, bf16[224,1024]{1,0:T(8,128)(2,1)}, bf16[896,128]{1,0:T(8,128)(2,1)S(1)}, f32[896,128]{1,0:T(8,128)S(1)}) %tuple.17), branch_computations={%region_0.1_spmd, %region_1.4_spmd} | conditional | flops 2896759040 | bytes 22182288 | solution.py:99
  24.0 2.5 %fusion = (f32[8,224]{1,0:T(8,128)S(1)}, f32[896,224,8]{0,1,2:T(8,128)S(1)}) fusion(pred[224,896]{1,0:T(8,128)(4,1)S(1)} %broadcast_compare_fusion, bf16[896,128]{1,0:T(8,128)(2,1)S(1)} %get-tuple-element.13, bf16[224,1024]{1,0:T(8,128)(2,1)} %get-tuple-element.23), kind=kOutput, calls=%fused_computation.2 | convolution fusion | flops 415856896 | bytes 7318528 | tf_op jit(solution)/shard_map/cond/branch_1_fun/rhd,nd->hrn/dot_general | solution.py:83
  26.5 6.8 %fusion.1 = f32[8,224,128]{2,1,0:T(8,128)S(1)} fusion(f32[896,224,8]{0,1,2:T(8,128)S(1)} %get-tuple-element.27, f32[8,224]{1,0:T(8,128)S(1)} %broadcast_maximum_fusion, pred[224,896]{1,0:T(8,128)(4,1)S(1)} %broadcast_compare_fusion, f32[896,128]{1,0:T(8,128)S(1)} %get-tuple-element.15), kind=kOutput, calls=%fused_computation.3 | convolution fusion | flops 2472673280 | bytes 8006656 | tf_op jit(solution)/shard_map/cond/branch_1_fun/hrn,nd->hrd/dot_general | solution.py:93
  33.3 2.2 fusion.2
  35.7 12.8 %convolution_multiply_fusion = f32[224,8192]{1,0:T(8,128)} fusion(bf16[1024,8192]{1,0:T(8,128)(2,1)} %param.10, f32[8192]{0:T(1024)S(1)} %add_convert_fusion, f32[8,224,128]{2,1,0:T(8,128)S(1)} %get-tuple-element.20, f32[8,224]{1,0:T(8,128)S(1)} %get-tuple-element.21), kind=kOutput, calls=%fused_computation.22 | convolution fusion | flops 3760390144 | bytes 25074688 | tf_op jit(solution)/shard_map/dot_general | solution.py:121
  48.5 8.9 %reshape.89 = f32[14336,128]{1,0:T(8,128)} reshape(f32[224,8192]{1,0:T(8,128)} %convolution_multiply_fusion) | data formatting | bytes 14680064 | tf_op jit(solution)/shard_map/reshape | solution.py:29
  57.4 4.4 %fusion.20 = f32[14336,128]{0,1:T(8,128)S(1)} fusion(f32[14336,128]{1,0:T(8,128)} %reshape.89), kind=kOutput, calls=%fused_computation.30 | convolution fusion | flops 472170496 | bytes 14680064 | tf_op jit(solution)/shard_map/dot_general | solution.py:33
  62.6 4.0 %multiply_reduce_fusion = (f32[14336]{0:T(1024)S(1)}, f32[14336,128]{0,1:T(8,128)}) fusion(f32[14336,128]{0,1:T(8,128)S(1)} %fusion.20, f32[14336,128]{1,0:T(8,128)S(1)} %copy-done.2), kind=kOutput, calls=%fused_computation.27 | convolution fusion | flops 485001216 | bytes 22077440 | tf_op jit(solution)/shard_map/dot_general | solution.py:34
  66.5 8.7 %copy.20 = f32[14336,128]{1,0:T(8,128)} copy(f32[14336,128]{0,1:T(8,128)} %get-tuple-element.29) | data formatting | bytes 14680064 | tf_op jit(solution)/shard_map/mul | solution.py:35
  75.2 9.0 %reshape_reshape.3 = f32[224,8192]{1,0:T(8,128)} reshape(f32[14336,128]{1,0:T(8,128)} %copy.20) | data formatting | bytes 14680064 | tf_op jit(solution)/shard_map/reshape;reshape | solution.py:41
  84.3 4.3 %div.53 = f32[224,64,128]{2,1,0:T(8,128)} broadcast(f32[224,64]{1,0:T(8,128)S(1)} %mul.78), dimensions={0,1} | broadcast | bytes 7397376 | tf_op jit(solution)/shard_map/div | solution.py:44
  88.6 1.4 copy-done.3
  90.0 13.2 %bitcast_multiply_fusion = f32[224,8192]{1,0:T(8,128)} fusion(f32[28,8,64,128]{3,2,1,0:T(8,128)} %bitcast.54, f32[224,8192]{1,0:T(8,128)S(1)} %copy-done.3), kind=kLoop, calls=%fused_computation.23 | loop fusion | flops 9175040 | bytes 22020096 | tf_op jit(solution)/shard_map/mul | solution.py:124
  103.3 82.9 %reduce-scatter.2.cloned.1.call-done = f32[224,1024]{1,0:T(8,128)} async-done(((f32[224,8192]{1,0:T(8,128)}), f32[224,1024]{1,0:T(8,128)}) %reduce-scatter.2.cloned.1.call-update) | async-done | bytes 917520 | tf_op jit(solution)/shard_map/reduce_scatter | solution.py:125
  186.2 1.4 abs_bitcast_fusion
  188.4 1.0 fusion.22
  189.5 16.7 %all_gather.15 = bf16[224,64]{0,1:T(8,128)(2,1)S(1)} all-gather(bf16[224,8]{0,1:T(8,128)(2,1)S(1)} %copy.21), channel_id=1, replica_groups=mesh['ctx'=4,'tp'=8] {'tp'}, dimensions={1}, use_global_device_ids=true | all-gather | bytes 32256 | tf_op jit(solution)/shard_map/all_gather | solution.py:129
  206.8 26.3 %all-gather.2.cloned.1.call-done = bf16[224,8192]{1,0:T(8,128)(2,1)} async-done(((bf16[224,1024]{1,0:T(8,128)(2,1)}), bf16[224,8192]{1,0:T(8,128)(2,1)}) %all-gather.2.cloned.1.call-update) | async-done | bytes 3670032 | tf_op jit(solution)/shard_map/all_gather | solution.py:128
  233.2 4.3 %copy.47 = bf16[224,8192]{1,0:T(8,128)(2,1)} copy(bf16[224,8192]{1,0:T(8,128)(2,1)} %all-gather.2.cloned.1.call-done) | data formatting | bytes 7340032
  (27 shorter events, 3.3 us)
Async XLA Ops:
  7.2 1.0 copy-start
  7.2 179.0 %reduce-scatter.2.cloned.1.call-start = ((), (), s32[]{:S(2)}) async-start(), calls=%async_computation.1 | async-start | bytes 8257536 | tf_op jit(solution)/shard_map/reduce_scatter | solution.py:125
  57.4 5.2 %copy-start.2 = (f32[14336,128]{1,0:T(8,128)S(1)}, f32[14336,128]{1,0:T(8,128)}, u32[]{:S(2)}) copy-start(f32[14336,128]{1,0:T(8,128)} %reshape.89) | copy-start | bytes 22020100
  84.3 5.7 %copy-start.3 = (f32[224,8192]{1,0:T(8,128)S(1)}, f32[224,8192]{1,0:T(8,128)}, u32[]{:S(2)}) copy-start(f32[224,8192]{1,0:T(8,128)} %reshape_reshape.3) | copy-start | bytes 22020100
  103.3 129.9 %all-gather.2.cloned.1.call-start = ((), (), s32[]{:S(2)}) async-start(), calls=%async_computation.2 | async-start | bytes 4128768 | tf_op jit(solution)/shard_map/all_gather | solution.py:128
  186.2 2.2 copy-start.4
  187.6 49.8 %copy-start.1 = (bf16[224,1024]{1,0:T(8,128)(2,1)S(1)}, bf16[224,1024]{1,0:T(8,128)(2,1)}, u32[]{:S(2)}) copy-start(bf16[224,1024]{1,0:T(8,128)(2,1)} %param.9) | copy-start | bytes 1376260
Sparse Core Ops, SparseCore 0:
  103.4 82.7 reduce-scatter.1
  189.6 43.5 all-gather.1
where the time goes:
time: 246 us; the launch traced here: 244 us
  waiting for transfers between devices  109 us (44%)
  local copies, waits for them, and re-layouts  40.3 us (16%)
  matrix products  30.5 us (12%)
  blocking collectives  29.3 us (12%)
  other arithmetic  19.8 us (8%)
  between operations  14.8 us (6%)
    reduce_scatter x1, waiting for transfers between devices, local(): lax.psum_scatter(restored.reshape(row_count, D), 'tp', scatter_dimension=...  82.9 us
    all_gather x1, waiting for transfers between devices, local(): lax.all_gather(out_payload, 'tp', axis=1, tiled=True)  26.3 us
    all_gather x1, blocking collectives, local(): lax.all_gather(out_scales.astype(jnp.bfloat16), 'tp', axis=1, tiled=True)  16.7 us
    mul x1, other arithmetic, local(): payload.astype(jnp.float32).reshape(row_count, -1, BLOCK)  13.2 us
    dot_general x1, matrix products, local(): jnp.dot(attended, out_weight, preferred_element_type=jnp.float32)  12.8 us
    another operation x1, local copies, waits for them, and re-layouts, clip_quantize(): blocked = rotated.reshape(row_count, -1, BLOCK)  9.01 us
    reshape x1, local copies, waits for them, and re-layouts, rotate(): flat = (partial_value * sign_row[None, :]).reshape(-1, BLOCK)  8.9 us
    mul x1, local copies, waits for them, and re-layouts, rotate(): turned = turned * jnp.float32(1.0 / math.sqrt(BLOCK))  8.65 us
  transfers between devices with their start and end apart: 2, of which 2 were waited for; matrix products, arithmetic and copies ran while one was open for 0% of the time, Pallas kernels for 0%

commit v1 on v0

v1 whole, which is shorter than its diff:
```python
import functools
import math

import jax
import jax.numpy as jnp
from jax import lax
from jax.experimental import pallas as pl
from jax.experimental.pallas import tpu as pltpu
from jax.sharding import PartitionSpec as P

HEAD = 128
BLOCK = 128
CORES = 2
CHUNK = CORES * BLOCK
MID_SKEW = 2
HOP_SKEW = 7
MESH = pl.DeviceIdType.MESH
F32 = jnp.float32
BF16 = jnp.bfloat16


def kernel(
    n_ctx,
    n_tp,
    kv_group,
    q_hbm,
    k_hbm,
    v_hbm,
    w_hbm,
    sign_hbm,
    out_hbm,
    scale_hbm,
    q_ref,
    sign_ref,
    k_all,
    v_all,
    w_all,
    att,
    run_max,
    run_sum,
    run_acc,
    turn_ref,
    ones_ref,
    own,
    sib_out,
    sib_in,
    outer_in,
    mine,
    cross_in,
    total,
    sib_total,
    fin,
    scales,
    load_sem,
    w_sem,
    kv_send,
    kv_recv,
    sib_send,
    sib_recv,
    inward_send,
    outer_recv,
    cross_recv,
    outward_send,
    total_recv,
    share_send,
    share_recv,
    out_sem,
):
    rows, depth = q_ref.shape
    heads = depth // HEAD
    steps = w_all.shape[0]
    ctx = lax.axis_index("ctx")
    tp = lax.axis_index("tp")
    core = lax.rem(tp, CORES)
    chip = tp // CORES
    chips = n_tp // CORES
    half = chips // 2
    left = chip < half
    edge = jnp.where(left, chip, chips - 1 - chip)
    centre = edge == half - 1
    has_outer = edge > 0
    ahead = jnp.where(left, CORES, -CORES)
    sibling = tp + 1 - 2 * core
    inward = tp + ahead
    outward = tp - ahead

    head_at = tp * heads // kv_group
    cols = pl.ds(pl.multiple_of(head_at * HEAD, HEAD), HEAD)

    loads = [
        pltpu.make_async_copy(k_hbm.at[:, cols], k_all.at[ctx], load_sem.at[0]),
        pltpu.make_async_copy(q_hbm, q_ref, load_sem.at[1]),
        pltpu.make_async_copy(v_hbm.at[:, cols], v_all.at[ctx], load_sem.at[2]),
        pltpu.make_async_copy(sign_hbm, sign_ref, load_sem.at[3]),
    ]
    for load in loads:
        load.start()

    barrier = pltpu.get_barrier_semaphore()

    @pl.loop(1, n_ctx)
    def _(step):
        pl.semaphore_signal(
            barrier, inc=1, device_id=(lax.rem(ctx + step, n_ctx), tp), device_id_type=MESH
        )

    pl.semaphore_signal(barrier, inc=1, device_id=(ctx, sibling), device_id_type=MESH)
    pl.semaphore_signal(barrier, inc=1, device_id=(ctx, inward), device_id_type=MESH)

    @pl.when(has_outer)
    def _():
        pl.semaphore_signal(barrier, inc=1, device_id=(ctx, outward), device_id_type=MESH)

    pl.semaphore_wait(barrier, n_ctx + 1 + jnp.where(has_outer, 1, 0))

    def kv_copies(source, target):
        return [
            pltpu.make_async_remote_copy(
                src_ref=hbm.at[:, cols],
                dst_ref=gathered.at[source],
                send_sem=kv_send.at[which, target],
                recv_sem=kv_recv.at[which, source],
                device_id=(target, tp),
                device_id_type=MESH,
            )
            for which, (hbm, gathered) in enumerate(((k_hbm, k_all), (v_hbm, v_all)))
        ]

    @pl.loop(0, n_ctx - 1 - ctx)
    def _(step):
        for copy in kv_copies(ctx, n_ctx - 1 - step):
            copy.start()

    def w_copy(step):
        wide = pl.ds(pl.multiple_of(step * CHUNK, CHUNK), CHUNK)
        return pltpu.make_async_copy(w_hbm.at[:, wide], w_all.at[step], w_sem.at[step])

    @pl.loop(0, steps)
    def _(step):
        w_copy(step).start()

    row_id = lax.broadcasted_iota(jnp.int32, (CHUNK, CHUNK), 0)
    col_id = lax.broadcasted_iota(jnp.int32, (CHUNK, CHUNK), 1)
    same = (row_id // BLOCK) == (col_id // BLOCK)
    common = jnp.bitwise_and(jnp.bitwise_and(row_id, col_id), BLOCK - 1)
    parity = jnp.zeros((CHUNK, CHUNK), jnp.int32)
    for bit in range(BLOCK.bit_length() - 1):
        parity = jnp.bitwise_xor(parity, jnp.right_shift(common, bit))
    odd = jnp.bitwise_and(parity, 1)
    turn_ref[...] = jnp.where(same, (1 - 2 * odd).astype(F32), 0.0).astype(BF16)
    ones_ref[...] = jnp.where(same, 1.0, 0.0).astype(BF16)
    scales[...] = jnp.zeros_like(scales)

    for load in loads:
        load.wait()

    exponent = math.log2(math.e) / math.sqrt(HEAD)

    def absorb(source, diagonal):
        key = k_all[source]
        value_t = v_all[source].astype(F32).T.astype(BF16)
        for h in range(heads):
            query = q_ref[:, h * HEAD : (h + 1) * HEAD]
            scores = lax.dot_general(
                key, query, (((1,), (1,)), ((), ())), preferred_element_type=F32
            )
            scores = scores * exponent
            if diagonal:
                key_pos = lax.broadcasted_iota(jnp.int32, (rows, rows), 0)
                query_pos = lax.broadcasted_iota(jnp.int32, (rows, rows), 1)
                scores = jnp.where(key_pos <= query_pos, scores, -1e30)
            top = jnp.max(scores, axis=0, keepdims=True)
            if not diagonal:
                before = run_max[h]
                top = jnp.maximum(before, top)
                keep = jnp.exp2(before - top)
            weights = jnp.exp2(scores - top)
            weight_sum = jnp.sum(weights, axis=0, keepdims=True)
            mixed = jnp.dot(value_t, weights.astype(BF16), preferred_element_type=F32)
            if not diagonal:
                weight_sum = weight_sum + keep * run_sum[h]
                mixed = mixed + keep * run_acc[h]
            run_max[h] = top
            run_sum[h] = weight_sum
            run_acc[h] = mixed

    absorb(ctx, True)

    @pl.loop(1, ctx + 1)
    def _(back):
        source = ctx - back
        for copy in kv_copies(source, ctx):
            copy.wait_recv()
        absorb(source, False)

    for h in range(heads):
        normed = run_acc[h] / run_sum[h]
        att[:, h * HEAD : (h + 1) * HEAD] = normed.T.astype(BF16)

    def remote(src, dst, send, recv, target):
        return pltpu.make_async_remote_copy(
            src_ref=src,
            dst_ref=dst,
            send_sem=send,
            recv_sem=recv,
            device_id=(ctx, target),
            device_id_type=MESH,
        )

    def sib_copy(k):
        return remote(sib_out.at[k], sib_in.at[k], sib_send.at[k], sib_recv.at[k], sibling)

    def outer_copy(k):
        return remote(mine.at[k], outer_in.at[k], inward_send.at[k], outer_recv.at[k], inward)

    def cross_copy(k):
        return remote(mine.at[k], cross_in.at[k], inward_send.at[k], cross_recv.at[k], inward)

    def total_copy(k):
        return remote(total.at[k], total.at[k], outward_send.at[k], total_recv.at[k], outward)

    def share_copy(k):
        return remote(total.at[k], sib_total.at[k], share_send.at[k], share_recv.at[k], sibling)

    def out_copy(k):
        wide = pl.ds(pl.multiple_of(k * CHUNK, CHUNK), CHUNK)
        return pltpu.make_async_copy(fin.at[k], out_hbm.at[:, wide], out_sem.at[k])

    def project(k):
        w_copy(k).wait()
        part = jnp.dot(att[...], w_all[k], preferred_element_type=F32)
        sign_row = jnp.concatenate(
            [sign_ref[pl.ds(k * CORES + i, 1), :] for i in range(CORES)], axis=1
        )
        part = part * (2 * sign_row - 1).astype(F32)
        turned = jnp.dot(part.astype(BF16), turn_ref[...], preferred_element_type=F32)
        turned = turned * F32(1.0 / math.sqrt(BLOCK))
        squares = jnp.dot((part * part).astype(BF16), ones_ref[...], preferred_element_type=F32)
        limit = 2.0 * jnp.sqrt(squares * F32(1.0 / BLOCK) + 1e-06)
        clipped = jnp.clip(turned, -limit, limit)
        low, high = clipped[:, :BLOCK], clipped[:, BLOCK:]
        sib_out[k] = jnp.where(core == 0, high, low).astype(BF16)
        sib_copy(k).start()
        own[k] = jnp.where(core == 0, low, high)

    def gather_in(k):
        sib_copy(k).wait_recv()
        pair = own[k] + sib_in[k].astype(F32)

        @pl.when(has_outer)
        def _():
            outer_copy(k).wait_recv()
            mine[k] = (pair + outer_in[k].astype(F32)).astype(BF16)

        @pl.when(jnp.logical_not(has_outer))
        def _():
            mine[k] = pair.astype(BF16)

        @pl.when(centre)
        def _():
            cross_copy(k).start()

        @pl.when(jnp.logical_not(centre))
        def _():
            outer_copy(k).start()

    lane = lax.broadcasted_iota(jnp.int32, scales.shape, 1)

    def finish(k, which, summed):
        summed = summed.astype(F32)
        scale = jnp.max(jnp.abs(summed), axis=1, keepdims=True) + 1e-06
        payload = (summed * (1.0 / scale)).astype(BF16)
        fin[k, :, pl.ds(pl.multiple_of(which * BLOCK, BLOCK), BLOCK)] = payload
        scales[...] = jnp.where(lane == k * CORES + which, scale, scales[...])

    def spread(k):
        @pl.when(centre)
        def _():
            cross_copy(k).wait_recv()
            total[k] = (mine[k].astype(F32) + cross_in[k].astype(F32)).astype(BF16)

        @pl.when(jnp.logical_not(centre))
        def _():
            total_copy(k).wait_recv()

        @pl.when(has_outer)
        def _():
            total_copy(k).start()

        share_copy(k).start()
        finish(k, core, total[k])

    def close(k):
        share_copy(k).wait_recv()
        finish(k, 1 - core, sib_total[k])
        out_copy(k).start()

    skew = MID_SKEW + HOP_SKEW * (half - 1 - edge)

    @pl.loop(0, steps + 2 + skew)
    def _(step):
        @pl.when(step < steps)
        def _():
            project(step)

        @pl.when(jnp.logical_and(step >= 1, step < steps + 1))
        def _():
            gather_in(step - 1)

        @pl.when(jnp.logical_and(step >= 1 + skew, step < steps + 1 + skew))
        def _():
            spread(step - 1 - skew)

        @pl.when(step >= 2 + skew)
        def _():
            close(step - 2 - skew)

    scale_copy = pltpu.make_async_copy(scales, scale_hbm, load_sem.at[0])
    scale_copy.start()

    @pl.loop(0, n_ctx - 1 - ctx)
    def _(step):
        for copy in kv_copies(ctx, n_ctx - 1 - step):
            copy.wait_send()

    @pl.loop(0, steps)
    def _(k):
        sib_copy(k).wait_send()
        outer_copy(k).wait_send()
        share_copy(k).wait_send()
        out_copy(k).wait()

        @pl.when(has_outer)
        def _():
            total_copy(k).wait_send()

    scale_copy.wait()


def local(n_ctx, n_tp, queries, keys, values, out_weight, signs):
    rows, depth = queries.shape
    width = out_weight.shape[1]
    heads = depth // HEAD
    kv_group = heads * n_tp // (keys.shape[1] // HEAD)
    steps = width // CHUNK
    blocks = width // BLOCK
    piece = pltpu.VMEM((steps, rows, BLOCK), BF16)
    per_step = pltpu.SemaphoreType.DMA((steps,))
    any_spec = pl.BlockSpec(memory_space=pl.ANY)
    flops = 2 * rows * width * (depth + 2 * CHUNK) + 4 * rows * rows * n_ctx * depth
    return pl.pallas_call(
        functools.partial(kernel, n_ctx, n_tp, kv_group),
        out_shape=(
            jax.ShapeDtypeStruct((rows, width), BF16),
            jax.ShapeDtypeStruct((rows, blocks), F32),
        ),
        in_specs=[any_spec] * 5,
        out_specs=(any_spec, any_spec),
        scratch_shapes=[
            pltpu.VMEM((rows, depth), BF16),
            pltpu.VMEM((blocks, BLOCK), jnp.int32),
            pltpu.VMEM((n_ctx, rows, HEAD), BF16),
            pltpu.VMEM((n_ctx, rows, HEAD), BF16),
            pltpu.VMEM((steps, depth, CHUNK), BF16),
            pltpu.VMEM((rows, depth), BF16),
            pltpu.VMEM((heads, 1, rows), F32),
            pltpu.VMEM((heads, 1, rows), F32),
            pltpu.VMEM((heads, HEAD, rows), F32),
            pltpu.VMEM((CHUNK, CHUNK), BF16),
            pltpu.VMEM((CHUNK, CHUNK), BF16),
            pltpu.VMEM((steps, rows, BLOCK), F32),
            piece,
            piece,
            piece,
            piece,
            piece,
            piece,
            piece,
            pltpu.VMEM((steps, rows, CHUNK), BF16),
            pltpu.VMEM((rows, blocks), F32),
            pltpu.SemaphoreType.DMA((4,)),
            per_step,
            pltpu.SemaphoreType.DMA((2, n_ctx)),
            pltpu.SemaphoreType.DMA((2, n_ctx)),
            per_step,
            per_step,
            per_step,
            per_step,
            per_step,
            per_step,
            per_step,
            per_step,
            per_step,
            per_step,
        ],
        compiler_params=pltpu.CompilerParams(
            collective_id=0, has_side_effects=True, vmem_limit_bytes=54 * 1024 * 1024
        ),
        cost_estimate=pl.CostEstimate(
            flops=flops, bytes_accessed=2 * depth * width + 4 * rows * width, transcendentals=0
        ),
    )(queries, keys, values, out_weight, signs.reshape(blocks, BLOCK))


def solution(mesh):
    n_ctx, n_tp = mesh.shape["ctx"], mesh.shape["tp"]
    return jax.shard_map(
        functools.partial(local, n_ctx, n_tp),
        mesh=mesh,
        in_specs=(P("ctx", "tp"), P("ctx", None), P("ctx", None), P("tp", None), P()),
        out_specs=(P("ctx", None), P("ctx", None)),
        check_vma=False,
    )
```

time: 246 us -> 79.1 us (0.32)
  waiting for transfers between devices: 109 us -> 0 us
  Pallas kernels: 0 us -> 72.5 us
  local copies, waits for them, and re-layouts: 40.3 us -> 5.87 us
  matrix products: 30.5 us -> 0 us
  blocking collectives: 29.3 us -> 0 us
  other arithmetic: 19.8 us -> 0 us
  between operations: 14.8 us -> 0.64 us
    reduce_scatter x1 -> x0, waiting for transfers between devices: 82.9 us -> none  [local(): lax.psum_scatter(restored.reshape(row_count, D), 'tp', scatter_dimension=...]
    pallas_call x0 -> x1, Pallas kernels: none -> 72.5 us  [local(): pl.pallas_call(functools.partial(kernel, n_ctx, n_tp, kv_group), out_shap...]
    dot_general x5 -> x0, matrix products: 30.5 us -> none  [the longest x1 12.8 us: local(): jnp.dot(attended, out_weight, preferred_element_type=jnp.float32)]
    all_gather x3 -> x0, blocking collectives: 29.3 us -> none  [the longest x1 16.7 us: local(): lax.all_gather(out_scales.astype(jnp.bfloat16), 'tp', axis=1, tiled=True)]
    all_gather x1 -> x0, waiting for transfers between devices: 26.3 us -> none  [local(): lax.all_gather(out_payload, 'tp', axis=1, tiled=True)]
    mul x2 -> x0, other arithmetic: 13.3 us -> none  [the longest x1 13.2 us: local(): payload.astype(jnp.float32).reshape(row_count, -1, BLOCK)]
    another operation x1 -> x0, local copies, waits for them, and re-layouts: 9.01 us -> none  [clip_quantize(): blocked = rotated.reshape(row_count, -1, BLOCK)]
    reshape x1 -> x0, local copies, waits for them, and re-layouts: 8.9 us -> none  [rotate(): flat = (partial_value * sign_row[None, :]).reshape(-1, BLOCK)]
  transfers between devices with their start and end apart: 2 -> 0, of which waited for: 2 -> 0; matrix products, arithmetic and copies ran while one was open for 0% -> 0% of each run, Pallas kernels for 0% -> 0%
where the time goes in v1:
time: 79.1 us; the launch traced here: 79 us
  Pallas kernels  72.5 us (92%)
  local copies, waits for them, and re-layouts  5.87 us (7%)
    pallas_call x1, Pallas kernels, local(): pl.pallas_call(functools.partial(kernel, n_ctx, n_tp, kv_group), out_shap...  72.5 us
    unnamed x1, local copies, waits for them, and re-layouts  4.26 us
    pallas_call x1, local copies, waits for them, and re-layouts, local(): pl.pallas_call(functools.partial(kernel, n_ctx, n_tp, kv_group), out_shap...  1.61 us

profile of v1, /device:TPU:7, one launch (start us, length us, event | category | flops | bytes accessed | tf_op | source)
XLA Modules:
  0.0 79.0 jit_solution(3421608710290272489)
XLA Ops:
  0.6 72.5 %shard_map.68 = (bf16[224,8192]{1,0:T(8,128)(2,1)}, f32[224,64]{1,0:T(8,128)}) custom-call(bf16[224,1024]{1,0:T(8,128)(2,1)} %q_hbm.1, bf16[224,1024]{1,0:T(8,128)(2,1)} %k_hbm.1, bf16[224,1024]{1,0:T(8,128)(2,1)} %v_hbm.1, bf16[1024,8192]{1,0:T(8,128)(2,1)} %w_hbm.1, s32[64,128]{1,0:T(8,128)} %bitcast.1), custom_call_target="tpu_custom_call" | custom-call | flops 6459228160 | bytes 24117248 | tf_op jit(solution)/shard_map/pallas_call | solution.py:351
  73.1 1.6 %copy.7 = f32[224,64]{0,1:T(8,128)} copy(f32[224,64]{1,0:T(8,128)} %get-tuple-element.3) | data formatting | bytes 114688 | tf_op jit(solution)/shard_map/pallas_call | solution.py:351
  74.7 4.3 %copy.9 = bf16[224,8192]{1,0:T(8,128)(2,1)} copy(bf16[224,8192]{1,0:T(8,128)(2,1)} %get-tuple-element.6) | data formatting | bytes 7340032
